TPU v7x, 32 devices: a whole 2x2x4 slice. The times are simulated.
32 devices in a mesh: expert: 4 (over y, x), rep: 8 (over z, core).
Axes of the slice: x: 2, y: 2, z: 4, core: 2. Of those that a mesh axis runs over, the one named last changes fastest.
Arguments:
- route_ids: int32 [256, 2], P(('expert', 'rep')), may hold values from 0 to 3, all different within a row; in each aligned block of 8 rows (0 to 7, 8 to 15, ...) at most 4 rows name the same one
- route_weight: float32 [256, 2], P(('expert', 'rep')), may hold values from 0.2 to 0.8
- input_float: bfloat16 [256, 4096], P(('expert', 'rep')), may hold values from -6 to 6
- input_quant: bfloat16 [256, 4096], P(('expert', 'rep')), may hold values from -6 to 6
- keep_mask: int32 [256, 4096], P(('expert', 'rep')), may hold values 0 or 1
- grad_mixed: bfloat16 [256, 4096], P(('expert', 'rep')), may hold values from -192 to 192
- gate_weight: bfloat16 [4, 4096, 7168], P('expert', None, 'rep'), may hold values from -0.09375 to 0.09375
- up_weight: bfloat16 [4, 4096, 7168], P('expert', None, 'rep'), may hold values from -0.09375 to 0.09375
- down_base: bfloat16 [4, 7168, 4096], P('expert', 'rep'), may hold values from -0.0625 to 0.0625
- down_round: bfloat16 [4, 7168, 4096], P('expert', 'rep'), may hold values from -8 to 8
- down_step: float32 [4, 4096], P('expert'), may hold values from 0.004 to 0.04
Outputs:
- mixed: bfloat16 [256, 4096], P(('expert', 'rep'))
- round_grad: float32 [4, 7168, 4096], P('expert', 'rep')
Inputs may be any that keep to these rules, and one draw needn't show every extreme that they name: `route_ids`: within the 8 tokens of one device, each expert is named by at most 4 pairs; the two experts of a token differ.
All inputs are finite; a program needn't handle non-finite values. No bound on the sum of `keep_mask` on one device may be relied on, other than what follows from the above.
Results may differ from a plain program's by a relative error of at most 0.0065.
Values may be sent and summed in bfloat16 or wider, within the bound.
A program may use at most 128 MiB of HBM per device.

v0:
```python
import jax
import jax.numpy as jnp
from jax import lax
from jax.sharding import PartitionSpec as P


def local_slots(route_ids, experts):
    count = route_ids.shape[0]
    flat = route_ids.reshape(count * 2)
    onehot = (flat[:, None] == jnp.arange(experts, dtype=jnp.int32)[None, :]).astype(jnp.int32)
    before = jnp.cumsum(onehot, axis=0) - onehot
    return jnp.sum(before * onehot, axis=1).reshape(count, 2)


def body(
    route_ids,
    route_weight,
    input_float,
    input_quant,
    keep_mask,
    grad_mixed,
    gate_weight,
    up_weight,
    down_base,
    down_round,
    down_step,
):
    experts = lax.axis_size("expert")
    count = route_ids.shape[0]
    capacity = count // 2
    slot = local_slots(route_ids, experts)
    target = route_ids * capacity + slot
    columns = jnp.arange(experts * capacity, dtype=jnp.int32)
    first = (target[:, 0:1] == columns[None, :]).astype(jnp.float32)
    second = (target[:, 1:2] == columns[None, :]).astype(jnp.float32)
    placing = (first + second).astype(jnp.bfloat16)
    weighting = route_weight[:, 0:1] * first + route_weight[:, 1:2] * second
    x_in = jnp.where(keep_mask == 1, input_quant, input_float)
    send_rows = lax.dot_general(
        placing, x_in, (((0,), (0,)), ((), ())), preferred_element_type=jnp.float32
    ).astype(jnp.bfloat16)
    send_cot = lax.dot_general(
        weighting,
        grad_mixed.astype(jnp.float32),
        (((0,), (0,)), ((), ())),
        precision=lax.Precision.HIGHEST,
        preferred_element_type=jnp.float32,
    ).astype(jnp.bfloat16)
    own_rows, own_cot = (
        lax.all_to_all(send_rows, "expert", split_axis=0, concat_axis=0, tiled=True),
        lax.all_to_all(send_cot, "expert", split_axis=0, concat_axis=0, tiled=True),
    )
    w_gate = gate_weight[0]
    w_up = up_weight[0]
    soft = jax.nn.sigmoid(down_round[0].astype(jnp.float32))
    step_row = down_step[0][None, :]
    quant_down = (down_base[0].astype(jnp.float32) + step_row * soft).astype(jnp.bfloat16)
    all_rows, all_cot = (
        lax.all_gather(own_rows, "rep", axis=0, tiled=True),
        lax.all_gather(own_cot, "rep", axis=0, tiled=True),
    )
    gate = jnp.dot(all_rows, w_gate, preferred_element_type=jnp.float32)
    up = jnp.dot(all_rows, w_up, preferred_element_type=jnp.float32)
    hidden = (jax.nn.silu(gate) * up).astype(jnp.bfloat16)
    grad_w = lax.dot_general(
        hidden, all_cot, (((0,), (0,)), ((), ())), preferred_element_type=jnp.float32
    )
    summed = lax.psum_scatter(
        jnp.dot(hidden, quant_down, preferred_element_type=jnp.float32),
        "rep",
        scatter_dimension=0,
        tiled=True,
    ).astype(jnp.bfloat16)
    returned = lax.all_to_all(summed, "expert", split_axis=0, concat_axis=0, tiled=True)
    mixed = jnp.dot(
        weighting,
        returned.astype(jnp.float32),
        precision=lax.Precision.HIGHEST,
        preferred_element_type=jnp.float32,
    ).astype(jnp.bfloat16)
    round_grad = (grad_w * step_row * soft * (1.0 - soft))[None]
    return (mixed, round_grad)


def solution(mesh):
    return jax.shard_map(
        body,
        mesh=mesh,
        in_specs=(
            P(("expert", "rep"), None),
            P(("expert", "rep"), None),
            P(("expert", "rep"), None),
            P(("expert", "rep"), None),
            P(("expert", "rep"), None),
            P(("expert", "rep"), None),
            P("expert", None, "rep"),
            P("expert", None, "rep"),
            P("expert", "rep", None),
            P("expert", "rep", None),
            P("expert", None),
        ),
        out_specs=(P(("expert", "rep"), None), P("expert", "rep", None)),
        check_vma=False,
    )
```

profile of v0, /device:TPU:0, one launch (start us, length us, event | category | flops | bytes accessed | tf_op | source)
XLA Modules:
  0.0 134.5 jit_solution(1344505090389268776)
XLA Ops:
  7.2 0.0 all-gather.3.cloned.1.call-start
  7.2 0.8 copy.15
  8.0 0.1 eq.51
  8.1 0.1 fusion.18
  8.2 0.2 select_reduce_fusion
  8.4 0.1 reshape.21
  8.4 0.2 slice_reduce_fusion.1
  8.6 1.3 convolution_convert_fusion.1
  9.9 0.1 all_to_all.24
  10.0 10.0 %all_to_all.36 = bf16[4,4,4096]{2,1,0:T(4,128)(2,1)S(1)} all-to-all(bf16[4,4,4096]{2,1,0:T(4,128)(2,1)S(1)} %all_to_all.24), channel_id=1, replica_groups=mesh['expert'=4,'rep'=8] {'expert'}, dimensions={0} | all-to-all | bytes 262144 | tf_op jit(solution)/shard_map/all_to_all | solution.py:50
  20.0 0.7 all_to_all.26
  20.7 0.0 all-gather.3.cloned.1.call-update
  20.7 0.0 reduce-scatter.2.cloned.1.call-start
  20.7 21.9 %all-gather.3.cloned.1.call-done = bf16[128,4096]{1,0:T(8,128)(2,1)} async-done(((bf16[16,4096]{1,0:T(8,128)(2,1)}), bf16[128,4096]{1,0:T(8,128)(2,1)}) %all-gather.3.cloned.1.call-update) | async-done | bytes 1048592 | tf_op jit(solution)/shard_map/all_gather | solution.py:59
  42.7 4.8 %fusion.8 = f32[128,896]{1,0:T(8,128)S(1)} fusion(bf16[128,4096]{1,0:T(8,128)(2,1)} %all-gather.3.cloned.1.call-done, bf16[1,4096,896]{2,1,0:T(8,128)(2,1)} %param.17), kind=kOutput, calls=%fused_computation.12 | convolution fusion | flops 939524096 | bytes 8847360 | tf_op jit(solution)/shard_map/dot_general | solution.py:62
  47.5 1.0 copy-done.3
  48.5 1.3 fusion.14
  49.8 9.2 %fusion.3 = f32[128,4096]{1,0:T(8,128)} fusion(bf16[128,896]{1,0:T(8,128)(2,1)S(1)} %fusion.14, bf16[1,896,4096]{2,1,0:T(8,128)(2,1)} %param.19, f32[4096]{0:T(1024)S(1)} %bitcast.43, bf16[1,896,4096]{2,1,0:T(8,128)(2,1)} %param.20), kind=kOutput, calls=%fused_computation.8 | convolution fusion | flops 968884224 | bytes 17022976 | tf_op jit(solution)/shard_map/dot_general | solution.py:69
  59.0 0.0 reduce-scatter.2.cloned.1.call-update
  59.0 0.0 all-gather.5.cloned.1.call-start
  59.1 0.4 convolution_convert_fusion
  59.5 0.1 all_to_all.30
  59.6 8.5 %all_to_all.37 = bf16[4,4,4096]{2,1,0:T(4,128)(2,1)S(1)} all-to-all(bf16[4,4,4096]{2,1,0:T(4,128)(2,1)S(1)} %all_to_all.30), channel_id=1, replica_groups=mesh['expert'=4,'rep'=8] {'expert'}, dimensions={0} | all-to-all | bytes 262144 | tf_op jit(solution)/shard_map/all_to_all | solution.py:51
  68.0 0.7 all_to_all.32
  68.7 0.0 all-gather.5.cloned.1.call-update
  68.7 25.8 %reduce-scatter.2.cloned.1.call-done = f32[16,4096]{1,0:T(8,128)} async-done(((f32[128,4096]{1,0:T(8,128)}), f32[16,4096]{1,0:T(8,128)}) %reduce-scatter.2.cloned.1.call-update) | async-done | bytes 262160 | tf_op jit(solution)/shard_map/reduce_scatter | solution.py:68
  94.6 1.0 convert_element_type.52
  95.5 0.7 all_to_all.27
  96.2 3.7 %all-to-all-start.1 = ((bf16[4,4,4096]{2,1,0:T(4,128)(2,1)}), bf16[4,4,4096]{2,1,0:T(4,128)(2,1)S(1)}, u32[]{:S(2)}, u32[]{:S(2)}) async-start(bf16[4,4,4096]{2,1,0:T(4,128)(2,1)} %all_to_all.27), calls=%async_computation.2 | async-start | bytes 262144 | tf_op jit(solution)/shard_map/all_to_all | solution.py:74
  99.9 17.1 %all-gather.5.cloned.1.call-done = bf16[128,4096]{1,0:T(8,128)(2,1)} async-done(((bf16[16,4096]{1,0:T(8,128)(2,1)}), bf16[128,4096]{1,0:T(8,128)(2,1)}) %all-gather.5.cloned.1.call-update) | async-done | bytes 1048592 | tf_op jit(solution)/shard_map/all_gather | solution.py:60
  117.0 10.0 %fusion.2 = f32[1,896,4096]{2,1,0:T(8,128)} fusion(bf16[128,896]{1,0:T(8,128)(2,1)S(1)} %fusion.14, bf16[128,4096]{1,0:T(8,128)(2,1)} %all-gather.5.cloned.1.call-done, f32[4096]{0:T(1024)S(1)} %bitcast.44, bf16[1,896,4096]{2,1,0:T(8,128)(2,1)} %param.20), kind=kOutput, calls=%fused_computation.6 | convolution fusion | flops 968884224 | bytes 23314432 | tf_op jit(solution)/shard_map/dot_general | solution.py:65
  127.1 0.9 convolution_convert_fusion.2
  (14 shorter events, 0.1 us)
Async XLA Ops:
  7.2 51.9 %copy-start = (bf16[8,4096]{1,0:T(8,128)(2,1)S(1)}, bf16[8,4096]{1,0:T(8,128)(2,1)}, u32[]{:S(2)}) copy-start(bf16[8,4096]{1,0:T(8,128)(2,1)} %param.16) | copy-start | bytes 196612
  7.2 35.5 %all-gather.3.cloned.1.call-start = ((), (), s32[]{:S(2)}) async-start(), calls=%async_computation.4 | async-start | bytes 1179648 | tf_op jit(solution)/shard_map/all_gather | solution.py:59
  20.7 29.1 %copy-start.4 = (f32[1,4096]{1,0:T(1,128)S(1)}, f32[1,4096]{1,0:T(1,128)}, u32[]{:S(2)}) copy-start(f32[1,4096]{1,0:T(1,128)} %param.21) | copy-start | bytes 49156
  20.7 73.9 %reduce-scatter.2.cloned.1.call-start = ((), (), s32[]{:S(2)}) async-start(), calls=%async_computation.5 | async-start | bytes 2359296 | tf_op jit(solution)/shard_map/reduce_scatter | solution.py:68
  42.7 4.8 %copy-start.1 = (bf16[128,4096]{1,0:T(8,128)(2,1)S(1)}, bf16[128,4096]{1,0:T(8,128)(2,1)}, u32[]{:S(2)}) copy-start(bf16[128,4096]{1,0:T(8,128)(2,1)} %all-gather.3.cloned.1.call-done) | copy-start | bytes 3145732
  42.7 5.8 %copy-start.3 = (bf16[1,4096,896]{2,1,0:T(8,128)(2,1)S(1)}, bf16[1,4096,896]{2,1,0:T(8,128)(2,1)}, u32[]{:S(2)}) copy-start(bf16[1,4096,896]{2,1,0:T(8,128)(2,1)} %param.18) | copy-start | bytes 22020100
  49.8 9.3 %copy-start.2 = (f32[8,2]{0,1:T(2,128)S(1)}, f32[8,2]{0,1:T(2,128)}, u32[]{:S(2)}) copy-start(f32[8,2]{0,1:T(2,128)} %param.12) | copy-start | bytes 196
  59.0 58.0 %all-gather.5.cloned.1.call-start = ((), (), s32[]{:S(2)}) async-start(), calls=%async_computation.6 | async-start | bytes 1179648 | tf_op jit(solution)/shard_map/all_gather | solution.py:60
  96.2 30.8 %all-to-all-start.1 = ((bf16[4,4,4096]{2,1,0:T(4,128)(2,1)}), bf16[4,4,4096]{2,1,0:T(4,128)(2,1)S(1)}, u32[]{:S(2)}, u32[]{:S(2)}) async-start(bf16[4,4,4096]{2,1,0:T(4,128)(2,1)} %all_to_all.27), calls=%async_computation.2 | async-start | bytes 262144 | tf_op jit(solution)/shard_map/all_to_all | solution.py:74
Sparse Core Ops, SparseCore 0:
  20.8 21.8 all-gather.2
  59.1 35.3 reduce-scatter.1
  96.2 20.8 all-gather.4
where the time goes:
time: 135 us
  waiting for transfers between devices  64.9 us (48%)
  matrix products  27.9 us (21%)
  blocking collectives  18.4 us (14%)
  between operations  13.9 us (10%)
  local copies, waits for them, and re-layouts  4.36 us (3%)
  starting transfers between devices  3.78 us (3%)
    reduce_scatter x1, waiting for transfers between devices, body(): lax.psum_scatter(jnp.dot(hidden, quant_down, preferred_element_type=jnp.f...  25.8 us
    all_gather x1, waiting for transfers between devices, body(): lax.all_gather(own_rows, 'rep', axis=0, tiled=True)  21.9 us
    all_gather x1, waiting for transfers between devices, body(): lax.all_gather(own_cot, 'rep', axis=0, tiled=True)  17.1 us
    dot_general x1, matrix products, body(): lax.dot_general(hidden, all_cot, (((0,), (0,)), ((), ())), preferred_elem...  10 us
    all_to_all x1, blocking collectives, body(): lax.all_to_all(send_rows, 'expert', split_axis=0, concat_axis=0, tiled=True)  9.99 us
    dot_general x1, matrix products, body(): jnp.dot(hidden, quant_down, preferred_element_type=jnp.float32)  9.2 us
    all_to_all x1, blocking collectives, body(): lax.all_to_all(send_cot, 'expert', split_axis=0, concat_axis=0, tiled=True)  8.45 us
    dot_general x1, matrix products, body(): gate = jnp.dot(all_rows, w_gate, preferred_element_type=jnp.float32)  4.81 us
  transfers between devices with their start and end apart: 4, of which 3 were waited for; matrix products, arithmetic and copies ran while one was open for 8% of the time, Pallas kernels for 0%

commit v1 on v0

--- a/solution.py
+++ b/solution.py
@@ -1,7 +1,477 @@
+import functools
+
 import jax
 import jax.numpy as jnp
 from jax import lax
+from jax.experimental import pallas as pl
+from jax.experimental.pallas import tpu as pltpu
 from jax.sharding import PartitionSpec as P
+
+MESH = pl.DeviceIdType.MESH
+VMEM_LIMIT = 56 * 1024 * 1024
+F32 = jnp.float32
+BF16 = jnp.bfloat16
+
+
+def dot(a, b, dims=((1,), (0,)), precision=None):
+    return lax.dot_general(
+        a, b, (dims, ((), ())), precision=precision, preferred_element_type=F32
+    )
+
+
+def placing_of(ids, weights, member, capacity, lanes):
+    count = ids.shape[0]
+    span = 4 * capacity
+    column = lax.broadcasted_iota(jnp.int32, (count, lanes), 1)
+    expert = column // span
+    inside = column - expert * span
+    group = inside // capacity
+    slot = (inside - group * capacity).astype(F32)
+    first = ids[:, 0:1] == expert
+    second = ids[:, 1:2] == expert
+    named = first.astype(F32) + second.astype(F32)
+    earlier = lax.broadcasted_iota(jnp.int32, (count, count), 1) < lax.broadcasted_iota(
+        jnp.int32, (count, count), 0
+    )
+    before = dot(earlier.astype(F32), named)
+    here = (before == slot) & (group == member)
+    placing = jnp.where(here, named, 0.0)
+    weighting = jnp.where(here & first, weights[:, 0:1], 0.0) + jnp.where(
+        here & second, weights[:, 1:2], 0.0
+    )
+    return placing, weighting
+
+
+def stack_halves(rows):
+    half = rows.shape[1] // 2
+    return jnp.concatenate([rows[:, :half], rows[:, half:]], axis=0)
+
+
+def layer_kernel(
+    experts,
+    reps,
+    ids_ref,
+    wts_ref,
+    xf_ref,
+    xq_ref,
+    keep_ref,
+    grad_ref,
+    step_ref,
+    gate_hbm,
+    up_hbm,
+    base_hbm,
+    round_hbm,
+    mixed_ref,
+    hidden_ref,
+    cot_hbm,
+    wg,
+    wu,
+    quant,
+    rounding,
+    meta,
+    xs,
+    gs,
+    xz,
+    gz,
+    xsend,
+    gsend,
+    xr,
+    gr,
+    gacc,
+    uacc,
+    osend,
+    orecv,
+    oacc,
+    rs_send,
+    rs_recv,
+    ret_send,
+    ret,
+    load_sem,
+    send_sem,
+    recv_sem,
+):
+    me_e = lax.axis_index("expert")
+    me_r = lax.axis_index("rep")
+    core = lax.rem(me_r, 2)
+    chip = me_r // 2
+    chips = reps // 2
+    pairs = chips // 2
+    my_pair = chip // 2
+    my_low = lax.rem(chip, 2)
+    other_core = chip * 2 + 1 - core
+    count, width = xf_ref.shape
+    half = width // 2
+    quarter = half // 2
+    capacity = count // 2
+    lanes = meta.shape[2]
+    span = 4 * capacity
+    hidden_width = wg.shape[1]
+    counter = [0]
+
+    def rep_at(offset):
+        return lax.rem(me_r + offset, reps)
+
+    def expert_at(offset):
+        return lax.rem(me_e + offset, experts)
+
+    def chip_at(j, i):
+        return lax.rem(my_pair + j, pairs) * 2 + lax.rem(my_low + i, 2)
+
+    def remote(source, target, expert, rep):
+        index = counter[0]
+        counter[0] += 1
+        return pltpu.make_async_remote_copy(
+            src_ref=source,
+            dst_ref=target,
+            send_sem=send_sem.at[index],
+            recv_sem=recv_sem.at[index],
+            device_id={"expert": expert, "rep": rep},
+            device_id_type=MESH,
+        )
+
+    barrier = pltpu.get_barrier_semaphore()
+    peers = [(me_e, rep_at(k)) for k in range(1, reps)]
+    for k in range(1, experts):
+        peers += [(expert_at(k), me_r), (expert_at(k), other_core)]
+    for expert, rep in peers:
+        pl.semaphore_signal(
+            barrier, inc=1, device_id={"expert": expert, "rep": rep}, device_id_type=MESH
+        )
+
+    loads = [
+        pltpu.make_async_copy(source.at[0], target, load_sem.at[n])
+        for n, (source, target) in enumerate(
+            [(round_hbm, rounding), (base_hbm, quant), (gate_hbm, wg), (up_hbm, wu)]
+        )
+    ]
+    for load in loads:
+        load.start()
+
+    x_in = jnp.where(keep_ref[...] == 1, xq_ref[...].astype(F32), xf_ref[...].astype(F32))
+    xs[core] = stack_halves(x_in).astype(BF16)
+    gs[core] = stack_halves(grad_ref[...].astype(F32)).astype(BF16)
+    ids = ids_ref[...]
+    wts = wts_ref[...]
+    placing, weighting = placing_of(ids, wts, lax.rem(me_r, 4), capacity, lanes)
+    meta[me_r, 0:count, :] = placing
+    meta[me_r, count : 2 * count, :] = weighting
+
+    pl.semaphore_wait(barrier, len(peers))
+
+    x_pair = remote(xs.at[core], xs.at[core], me_e, other_core)
+    g_pair = remote(gs.at[core], gs.at[core], me_e, other_core)
+    x_pair.start()
+    g_pair.start()
+    metas = [remote(meta.at[me_r], meta.at[me_r], me_e, rep_at(k)) for k in range(1, reps)]
+    for copy in metas:
+        copy.start()
+
+    def quantise(start, stop):
+        @pl.loop(start, stop)
+        def _(n):
+            rows = pl.ds(pl.multiple_of(n * 16, 16), 16)
+            soft = jax.nn.sigmoid(rounding[rows, :].astype(F32))
+            quant[rows, :] = (quant[rows, :].astype(F32) + step_ref[...] * soft).astype(BF16)
+
+    def own_half(stacked):
+        parts = []
+        for c in range(2):
+            both = stacked[c].astype(F32)
+            parts.append(jnp.where(core == 0, both[:count], both[count:]))
+        return jnp.concatenate(parts, axis=0).astype(BF16)
+
+    chip_offsets = [(j, i) for j in range(pairs) for i in range(2) if (j, i) != (0, 0)]
+
+    def to_chips(blocks):
+        copies = {}
+        for j, i in chip_offsets:
+            copies[j, i] = remote(
+                blocks.at[chip], blocks.at[chip], me_e, chip_at(j, i) * 2 + core
+            )
+            copies[j, i].start()
+        return copies
+
+    x_pair.wait_recv()
+    xz[chip] = own_half(xs)
+    x_chips = to_chips(xz)
+    g_pair.wait_recv()
+    gz[chip] = own_half(gs)
+    g_chips = to_chips(gz)
+
+    for copy in metas:
+        copy.wait_recv()
+
+    loads[0].wait()
+    loads[1].wait()
+    chunks = hidden_width // 16
+    quantise(0, chunks // 4)
+
+    def placings(pair):
+        block = meta[pl.ds(pair * 4, 4)]
+        place = block[:, 0:count, :].reshape(4 * count, lanes)
+        weight = block[:, count:, :].reshape(4 * count, lanes)
+        return place, weight
+
+    def dispatch(j, blocks, copies, sent, received, weighted):
+        for i in range(2):
+            if (j, i) in copies:
+                copies[j, i].wait_recv()
+        pair = lax.rem(my_pair + pairs - j, pairs)
+        place, weight = placings(pair)
+        tokens = blocks[pl.ds(pair * 2, 2)].reshape(4 * count, half)
+        picked = dot(place.astype(BF16), tokens, ((0,), (0,)))[: experts * span]
+        if weighted:
+            scale = dot(
+                weight, jnp.ones((4 * count, 128), F32), ((0,), (0,)), lax.Precision.HIGHEST
+            )
+            picked = picked * scale[: experts * span, 0:1]
+        sent[pair] = picked.astype(BF16).reshape(experts, span, half)
+        flying = []
+        for k in range(1, experts):
+            expert = expert_at(k)
+            copy = remote(
+                sent.at[pair, expert], received.at[core, pair * experts + me_e], expert, me_r
+            )
+            copy.start()
+            flying.append(copy)
+        received[core, pair * experts + me_e] = sent[pair, me_e]
+        return pair, flying
+
+    def forward(pair, received):
+        blocks = received.at[core, pl.ds(pair * experts, experts)]
+        copy = remote(blocks, blocks, me_e, other_core)
+        copy.start()
+        return copy
+
+    flights = []
+    x_sent = []
+    for j in range(pairs):
+        x_sent.append(dispatch(j, xz, x_chips, xsend, xr, False))
+        quantise(chunks * (1 + j) // (2 + pairs), chunks * (2 + j) // (2 + pairs))
+    g_sent = [dispatch(j, gz, g_chips, gsend, gr, True) for j in range(pairs)]
+    x_forward = []
+    for pair, flying in x_sent:
+        for copy in flying:
+            copy.wait_recv()
+        x_forward.append(forward(pair, xr))
+    quantise(chunks * (1 + pairs) // (2 + pairs), chunks)
+
+    loads[2].wait()
+    loads[3].wait()
+    gacc[...] = jnp.zeros_like(gacc)
+    uacc[...] = jnp.zeros_like(uacc)
+    depth = min(512, half)
+
+    def gate_up(side):
+        @pl.loop(0, half // depth)
+        def _(k):
+            columns = pl.ds(pl.multiple_of(k * depth, depth), depth)
+            rows = pl.ds(pl.multiple_of(side * half + k * depth, depth), depth)
+            block = xr[side, :, :, columns].reshape(-1, depth)
+            gacc[...] += dot(block, wg[rows, :])
+            uacc[...] += dot(block, wu[rows, :])
+
+    gate_up(core)
+    for copy in x_forward:
+        copy.wait_recv()
+    gate_up(1 - core)
+    gate = gacc[...]
+    hidden = (gate / (1.0 + jnp.exp(-gate)) * uacc[...]).astype(BF16)
+    hidden_ref[...] = hidden
+
+    g_forward = []
+    for pair, flying in g_sent:
+        for copy in flying:
+            copy.wait_recv()
+        g_forward.append(forward(pair, gr))
+
+    def down(side, result):
+        @pl.loop(0, half // depth)
+        def _(k):
+            columns = pl.ds(pl.multiple_of(k * depth, depth), depth)
+            source = pl.ds(pl.multiple_of(side * half + k * depth, depth), depth)
+            result[:, columns] = dot(hidden_ref[...], quant[:, source]).astype(result.dtype)
+
+    down(1 - core, osend)
+    o_pair = remote(osend, orecv, me_e, other_core)
+    o_pair.start()
+    down(core, oacc)
+    for copy in g_forward:
+        copy.wait_recv()
+    cot_out = pltpu.make_async_copy(gr, cot_hbm, load_sem.at[4])
+    cot_out.start()
+    o_pair.wait_recv()
+    for z in range(chips):
+        rows = []
+        for e in range(experts):
+            start = (z // 2 * experts + e) * span + z % 2 * 2 * capacity
+            part = oacc[start : start + 2 * capacity, :]
+            block = start // span * span
+            got = orecv[block : block + span, :].astype(F32)
+            rows.append(part + got[start - block : start - block + 2 * capacity])
+        rs_send[z] = jnp.concatenate(rows, axis=0).astype(BF16)
+    rs_copies = []
+    for n, (j, i) in enumerate(chip_offsets):
+        there = chip_at(j, i)
+        copy = remote(rs_send.at[there], rs_recv.at[n], me_e, there * 2 + core)
+        copy.start()
+        rs_copies.append(copy)
+    total = rs_send[chip].astype(F32)
+    for n, copy in enumerate(rs_copies):
+        copy.wait_recv()
+        total = total + rs_recv[n].astype(F32)
+    for e in range(experts):
+        part = total[e * 2 * capacity : (e + 1) * 2 * capacity]
+        ret_send[e] = stack_halves(part).astype(BF16)
+    ret_copies = []
+    for k in range(experts):
+        expert = expert_at(k)
+        for rep in (me_r, other_core):
+            if k == 0 and rep is me_r:
+                continue
+            copy = remote(ret_send.at[expert], ret.at[core, me_e], expert, rep)
+            copy.start()
+            ret_copies.append(copy)
+    ret[core, me_e] = ret_send[me_e]
+    weightings = [
+        placing_of(ids, wts, 2 * q + core, capacity, lanes)[1][:, : experts * span]
+        for q in range(2)
+    ]
+    for copy in ret_copies:
+        copy.wait_recv()
+    for h in range(2):
+        rows = ret[h].astype(F32).reshape(experts * span, quarter)
+        for q in range(2):
+            start = h * half + q * quarter
+            mixed_ref[:, start : start + quarter] = dot(
+                weightings[q], rows, precision=lax.Precision.HIGHEST
+            ).astype(BF16)
+
+    cot_out.wait()
+    sent = [x_pair, g_pair, o_pair] + metas + x_forward + g_forward + rs_copies + ret_copies
+    sent += list(x_chips.values()) + list(g_chips.values())
+    for _, flying in x_sent + g_sent:
+        sent += flying
+    for copy in sent:
+        copy.wait_send()
+
+
+def round_kernel(hidden_ref, cot_ref, round_ref, step_ref, out_ref):
+    hidden = hidden_ref[...]
+    half = cot_ref.shape[3]
+    for h in range(2):
+        columns = slice(h * half, (h + 1) * half)
+        soft = jax.nn.sigmoid(round_ref[0, :, columns].astype(F32))
+        grad = dot(hidden, cot_ref[h].reshape(-1, half), ((0,), (0,)))
+        out_ref[0, :, columns] = grad * step_ref[:, columns] * soft * (1.0 - soft)
+
+
+def fused_body(
+    experts,
+    reps,
+    route_ids,
+    route_weight,
+    input_float,
+    input_quant,
+    keep_mask,
+    grad_mixed,
+    gate_weight,
+    up_weight,
+    down_base,
+    down_round,
+    down_step,
+):
+    count, width = input_float.shape
+    half = width // 2
+    hidden_width = gate_weight.shape[2]
+    capacity = count // 2
+    span = 4 * capacity
+    chips = reps // 2
+    pairs = chips // 2
+    rows = reps * experts * capacity
+    copies = 2 + (reps - 1) + 2 * (chips - 1) + 2 * pairs * (experts - 1)
+    copies += 2 * pairs + 1 + (chips - 1) + 2 * experts
+    vmem = pl.BlockSpec(memory_space=pltpu.VMEM)
+    anywhere = pl.BlockSpec(memory_space=pl.ANY)
+    mixed, hidden, cot = pl.pallas_call(
+        functools.partial(layer_kernel, experts, reps),
+        out_shape=(
+            jax.ShapeDtypeStruct((count, width), BF16),
+            jax.ShapeDtypeStruct((rows, hidden_width), BF16),
+            jax.ShapeDtypeStruct((2, pairs * experts, span, half), BF16),
+        ),
+        in_specs=[vmem] * 7 + [anywhere] * 4,
+        out_specs=(vmem, vmem, anywhere),
+        scratch_shapes=[
+            pltpu.VMEM((width, hidden_width), BF16),
+            pltpu.VMEM((width, hidden_width), BF16),
+            pltpu.VMEM((hidden_width, width), BF16),
+            pltpu.VMEM((hidden_width, width), BF16),
+            pltpu.VMEM((reps, 2 * count, 128), F32),
+            pltpu.VMEM((2, 2 * count, half), BF16),
+            pltpu.VMEM((2, 2 * count, half), BF16),
+            pltpu.VMEM((chips, 2 * count, half), BF16),
+            pltpu.VMEM((chips, 2 * count, half), BF16),
+            pltpu.VMEM((pairs, experts, span, half), BF16),
+            pltpu.VMEM((pairs, experts, span, half), BF16),
+            pltpu.VMEM((2, pairs * experts, span, half), BF16),
+            pltpu.VMEM((2, pairs * experts, span, half), BF16),
+            pltpu.VMEM((rows, hidden_width), F32),
+            pltpu.VMEM((rows, hidden_width), F32),
+            pltpu.VMEM((rows, half), BF16),
+            pltpu.VMEM((rows, half), BF16),
+            pltpu.VMEM((rows, half), F32),
+            pltpu.VMEM((chips, experts * 2 * capacity, half), BF16),
+            pltpu.VMEM((chips - 1, experts * 2 * capacity, half), BF16),
+            pltpu.VMEM((experts, span, half // 2), BF16),
+            pltpu.VMEM((2, experts, span, half // 2), BF16),
+            pltpu.SemaphoreType.DMA((5,)),
+            pltpu.SemaphoreType.DMA((copies,)),
+            pltpu.SemaphoreType.DMA((copies,)),
+        ],
+        compiler_params=pltpu.CompilerParams(
+            collective_id=0, has_side_effects=True, vmem_limit_bytes=VMEM_LIMIT
+        ),
+        cost_estimate=pl.CostEstimate(
+            flops=6 * rows * width * hidden_width,
+            bytes_accessed=8 * width * hidden_width,
+            transcendentals=width * hidden_width,
+        ),
+        name="layer",
+    )(
+        route_ids,
+        route_weight,
+        input_float,
+        input_quant,
+        keep_mask,
+        grad_mixed,
+        down_step,
+        gate_weight,
+        up_weight,
+        down_base,
+        down_round,
+    )
+    tile = 128
+    round_grad = pl.pallas_call(
+        round_kernel,
+        out_shape=jax.ShapeDtypeStruct((1, hidden_width, width), F32),
+        grid=(hidden_width // tile,),
+        in_specs=[
+            pl.BlockSpec((rows, tile), lambda n: (0, n)),
+            pl.BlockSpec((2, pairs * experts, span, half), lambda n: (0, 0, 0, 0)),
+            pl.BlockSpec((1, tile, width), lambda n: (0, n, 0)),
+            pl.BlockSpec((1, width), lambda n: (0, 0)),
+        ],
+        out_specs=pl.BlockSpec((1, tile, width), lambda n: (0, n, 0)),
+        compiler_params=pltpu.CompilerParams(vmem_limit_bytes=VMEM_LIMIT),
+        cost_estimate=pl.CostEstimate(
+            flops=2 * rows * width * hidden_width,
+            bytes_accessed=6 * width * hidden_width,
+            transcendentals=width * hidden_width,
+        ),
+        name="round_grad",
+    )(hidden, cot, down_round, down_step)
+    return (mixed, round_grad)
 
 
 def local_slots(route_ids, experts):
@@ -83,8 +553,24 @@
 
 
 def solution(mesh):
+    experts, reps = mesh.shape["expert"], mesh.shape["rep"]
+
+    def choose(*args):
+        count, width = args[2].shape
+        hidden_width = args[6].shape[2]
+        capacity = count // 2
+        rows = reps * experts * capacity
+        weights = 8 * width * hidden_width
+        buffers = rows * (8 * hidden_width + 26 * width)
+        fits = weights + buffers <= VMEM_LIMIT * 7 // 8
+        fits = fits and hidden_width % 128 == 0 and reps % 4 == 0
+        fits = fits and count % 8 == 0 and experts * 4 * capacity <= 128
+        if fits:
+            return fused_body(experts, reps, *args)
+        return body(*args)
+
     return jax.shard_map(
-        body,
+        choose,
         mesh=mesh,
         in_specs=(
             P(("expert", "rep"), None),

time: 135 us -> 64.9 us (0.48)
  waiting for transfers between devices: 64.9 us -> 0 us
  Pallas kernels: 0 us -> 59.9 us
  matrix products: 27.9 us -> 0 us
  blocking collectives: 18.4 us -> 0 us
  between operations: 13.9 us -> 0.65 us
  starting transfers between devices: 3.78 us -> 0 us
    pallas_call x0 -> x2, Pallas kernels: none -> 59.9 us  [the longest x1 47.7 us: fused_body(): pl.pallas_call(functools.partial(layer_kernel, experts, reps), out_shape=...]
    all_gather x2 -> x0, waiting for transfers between devices: 39 us -> none  [the longest x1 21.9 us: body(): lax.all_gather(own_rows, 'rep', axis=0, tiled=True)]
    dot_general x7 -> x0, matrix products: 27.9 us -> none  [the longest x1 10 us: body(): lax.dot_general(hidden, all_cot, (((0,), (0,)), ((), ())), preferred_elem...]
    reduce_scatter x1 -> x0, waiting for transfers between devices: 25.8 us -> none  [body(): lax.psum_scatter(jnp.dot(hidden, quant_down, preferred_element_type=jnp.f...]
    all_to_all x2 -> x0, blocking collectives: 18.4 us -> none  [the longest x1 9.99 us: body(): lax.all_to_all(send_rows, 'expert', split_axis=0, concat_axis=0, tiled=True)]
    all_to_all x1 -> x0, starting transfers between devices: 3.66 us -> none  [body(): lax.all_to_all(summed, 'expert', split_axis=0, concat_axis=0, tiled=True)]
    all_to_all x6 -> x0, local copies, waits for them, and re-layouts: 2.23 us -> none  [the longest x2 0.75 us: body(): lax.all_to_all(send_rows, 'expert', split_axis=0, concat_axis=0, tiled=True)]
    unnamed x11 -> x5, local copies, waits for them, and re-layouts: 1.77 us -> 3.32 us
  transfers between devices with their start and end apart: 4 -> 0, of which waited for: 3 -> 0; matrix products, arithmetic and copies ran while one was open for 8% -> 0% of each run, Pallas kernels for 0% -> 0%
where the time goes in v1:
time: 64.9 us; the launch traced here: 63.9 us
  Pallas kernels  59.9 us (92%)
  local copies, waits for them, and re-layouts  3.32 us (5%)
  between operations  0.65 us (1%)
    pallas_call x1, Pallas kernels, fused_body(): pl.pallas_call(functools.partial(layer_kernel, experts, reps), out_shape=...  47.7 us
    pallas_call x1, Pallas kernels, fused_body(): pl.pallas_call(round_kernel, out_shape=jax.ShapeDtypeStruct((1, hidden_wi...  12.3 us
    unnamed x5, local copies, waits for them, and re-layouts  3.32 us

profile of v1, /device:TPU:0, one launch (start us, length us, event | category | flops | bytes accessed | tf_op | source)
XLA Modules:
  0.0 63.9 jit_solution(15318814872296925364)
XLA Ops:
  0.6 1.3 %copy.13.ids_ref = s32[8,2]{1,0:T(8,128)} copy(s32[8,2]{0,1:T(2,128)} %param.11) | data formatting | bytes 128 | tf_op args[0]
  2.0 1.3 %copy.14.wts_ref = f32[8,2]{1,0:T(8,128)} copy(f32[8,2]{0,1:T(2,128)} %param.12) | data formatting | bytes 128 | tf_op args[1]
  3.3 47.7 %layer.1 = (bf16[8,4096]{1,0:T(8,128)(2,1)}, bf16[128,896]{1,0:T(8,128)(2,1)}, bf16[2,8,16,2048]{3,2,1,0:T(8,128)(2,1)}) custom-call(s32[8,2]{1,0:T(8,128)} %copy.13.ids_ref, f32[8,2]{1,0:T(8,128)} %copy.14.wts_ref, bf16[8,4096]{1,0:T(8,128)(2,1)} %xf_ref.1, bf16[8,4096]{1,0:T(8,128)(2,1)} %xq_ref.1, s32[8,4096]{1,0:T(8,128)} %keep_ref.1, ...), custom_call_target="tpu_custom_call" | custom-call | flops 2818572288 | bytes 29360128 | tf_op jit(solution)/shard_map/layer/pallas_call | solution.py:396
  51.0 0.0 copy-start
  51.0 12.3 %round_grad.1 = f32[1,896,4096]{2,1,0:T(8,128)} custom-call(bf16[128,896]{1,0:T(8,128)(2,1)} %get-tuple-element.6.hidden_ref, bf16[2,8,16,2048]{3,2,1,0:T(8,128)(2,1)} %get-tuple-element.7.cot_ref, bf16[1,896,4096]{2,1,0:T(8,128)(2,1)} %round_ref.1, f32[1,4096]{1,0:T(1,128)} %step_ref.3), custom_call_target="tpu_custom_call" | custom-call | flops 939524096 | bytes 22020096 | tf_op jit(solution)/shard_map/round_grad/pallas_call | solution.py:455
  63.3 0.0 copy-done
  63.3 0.6 copy.16
Async XLA Ops:
  51.0 12.3 %copy-start = (bf16[8,4096]{1,0:T(8,128)(2,1)S(1)}, bf16[8,4096]{1,0:T(8,128)(2,1)}, u32[]{:S(2)}) copy-start(bf16[8,4096]{1,0:T(8,128)(2,1)} %get-tuple-element.10) | copy-start | bytes 196612

commit v2 on v1

--- a/solution.py
+++ b/solution.py
@@ -64,6 +64,7 @@
     mixed_ref,
     hidden_ref,
     cot_hbm,
+    slope_hbm,
     wg,
     wu,
     quant,
@@ -82,10 +83,10 @@
     osend,
     orecv,
     oacc,
-    rs_send,
-    rs_recv,
     ret_send,
     ret,
+    mix_send,
+    mix_recv,
     load_sem,
     send_sem,
     recv_sem,
@@ -131,8 +132,7 @@
 
     barrier = pltpu.get_barrier_semaphore()
     peers = [(me_e, rep_at(k)) for k in range(1, reps)]
-    for k in range(1, experts):
-        peers += [(expert_at(k), me_r), (expert_at(k), other_core)]
+    peers += [(expert_at(k), me_r) for k in range(1, experts)]
     for expert, rep in peers:
         pl.semaphore_signal(
             barrier, inc=1, device_id={"expert": expert, "rep": rep}, device_id_type=MESH
@@ -144,14 +144,19 @@
             [(round_hbm, rounding), (base_hbm, quant), (gate_hbm, wg), (up_hbm, wu)]
         )
     ]
-    for load in loads:
-        load.start()
+    loads[0].start()
+    loads[1].start()
 
     x_in = jnp.where(keep_ref[...] == 1, xq_ref[...].astype(F32), xf_ref[...].astype(F32))
     xs[core] = stack_halves(x_in).astype(BF16)
     gs[core] = stack_halves(grad_ref[...].astype(F32)).astype(BF16)
-    ids = ids_ref[...]
-    wts = wts_ref[...]
+    eye = (
+        lax.broadcasted_iota(jnp.int32, (count, count), 0)
+        == lax.broadcasted_iota(jnp.int32, (count, count), 1)
+    ).astype(F32)
+    across = ((1,), (1,))
+    ids = dot(eye, ids_ref[...].astype(F32), across, lax.Precision.HIGHEST).astype(jnp.int32)
+    wts = dot(eye, wts_ref[...], across, lax.Precision.HIGHEST)
     placing, weighting = placing_of(ids, wts, lax.rem(me_r, 4), capacity, lanes)
     meta[me_r, 0:count, :] = placing
     meta[me_r, count : 2 * count, :] = weighting
@@ -171,7 +176,9 @@
         def _(n):
             rows = pl.ds(pl.multiple_of(n * 16, 16), 16)
             soft = jax.nn.sigmoid(rounding[rows, :].astype(F32))
-            quant[rows, :] = (quant[rows, :].astype(F32) + step_ref[...] * soft).astype(BF16)
+            scaled = step_ref[...] * soft
+            quant[rows, :] = (quant[rows, :].astype(F32) + scaled).astype(BF16)
+            rounding[rows, :] = (scaled * (1.0 - soft)).astype(BF16)
 
     def own_half(stacked):
         parts = []
@@ -196,13 +203,14 @@
     x_chips = to_chips(xz)
     g_pair.wait_recv()
     gz[chip] = own_half(gs)
-    g_chips = to_chips(gz)
 
     for copy in metas:
         copy.wait_recv()
 
     loads[0].wait()
     loads[1].wait()
+    loads[2].start()
+    loads[3].start()
     chunks = hidden_width // 16
     quantise(0, chunks // 4)
 
@@ -243,18 +251,21 @@
         copy.start()
         return copy
 
-    flights = []
     x_sent = []
     for j in range(pairs):
         x_sent.append(dispatch(j, xz, x_chips, xsend, xr, False))
+        if j == pairs - 1:
+            g_chips = to_chips(gz)
         quantise(chunks * (1 + j) // (2 + pairs), chunks * (2 + j) // (2 + pairs))
-    g_sent = [dispatch(j, gz, g_chips, gsend, gr, True) for j in range(pairs)]
     x_forward = []
     for pair, flying in x_sent:
         for copy in flying:
             copy.wait_recv()
         x_forward.append(forward(pair, xr))
     quantise(chunks * (1 + pairs) // (2 + pairs), chunks)
+    slope_out = pltpu.make_async_copy(rounding, slope_hbm, load_sem.at[5])
+    slope_out.start()
+    g_sent = [dispatch(0, gz, g_chips, gsend, gr, True)]
 
     loads[2].wait()
     loads[3].wait()
@@ -272,6 +283,7 @@
             uacc[...] += dot(block, wu[rows, :])
 
     gate_up(core)
+    g_sent += [dispatch(j, gz, g_chips, gsend, gr, True) for j in range(1, pairs)]
     for copy in x_forward:
         copy.wait_recv()
     gate_up(1 - core)
@@ -279,12 +291,6 @@
     hidden = (gate / (1.0 + jnp.exp(-gate)) * uacc[...]).astype(BF16)
     hidden_ref[...] = hidden
 
-    g_forward = []
-    for pair, flying in g_sent:
-        for copy in flying:
-            copy.wait_recv()
-        g_forward.append(forward(pair, gr))
-
     def down(side, result):
         @pl.loop(0, half // depth)
         def _(k):
@@ -296,74 +302,81 @@
     o_pair = remote(osend, orecv, me_e, other_core)
     o_pair.start()
     down(core, oacc)
+    o_pair.wait_recv()
+    returning = []
+    for j in range(pairs):
+        pair = lax.rem(my_pair + 1 + j, pairs)
+        rows = pl.ds(pl.multiple_of(pair * experts * span, experts * span), experts * span)
+        both = oacc[rows, :] + orecv[rows, :].astype(F32)
+        ret_send[pair] = both.astype(BF16).reshape(experts, span, half)
+        flying = []
+        for k in range(1, experts):
+            expert = expert_at(k)
+            copy = remote(ret_send.at[pair, expert], ret.at[pair, me_e], expert, me_r)
+            copy.start()
+            flying.append(copy)
+        ret[pair, me_e] = ret_send[pair, me_e]
+        returning.append((pair, flying))
+    g_forward = []
+    for pair, flying in g_sent:
+        for copy in flying:
+            copy.wait_recv()
+        g_forward.append(forward(pair, gr))
+    member = lax.rem(me_r, 4)
+    mix_copies = []
+    for j, (pair, flying) in enumerate(returning):
+        weight = placings(pair)[1][:, : experts * span]
+        parts = []
+        for _ in range(3):
+            parts.append(weight.astype(BF16))
+            weight = weight - parts[-1].astype(F32)
+        for copy in flying:
+            copy.wait_recv()
+        mix = dot(jnp.concatenate(parts, axis=0), ret[pair].reshape(experts * span, half))
+        mix = mix.reshape(3, 4 * count, half).sum(axis=0)
+        for d in range(4):
+            rows = mix[d * count : (d + 1) * count]
+            mix_send[pair, d] = stack_halves(rows).astype(BF16)
+        for i in range(4):
+            if (j, i) == (pairs - 1, 0):
+                mix_recv[me_r] = mix_send[my_pair, member]
+                continue
+            there = lax.rem(member + i, 4)
+            copy = remote(mix_send.at[pair, there], mix_recv.at[me_r], me_e, pair * 4 + there)
+            copy.start()
+            mix_copies.append(copy)
     for copy in g_forward:
         copy.wait_recv()
     cot_out = pltpu.make_async_copy(gr, cot_hbm, load_sem.at[4])
     cot_out.start()
-    o_pair.wait_recv()
-    for z in range(chips):
-        rows = []
-        for e in range(experts):
-            start = (z // 2 * experts + e) * span + z % 2 * 2 * capacity
-            part = oacc[start : start + 2 * capacity, :]
-            block = start // span * span
-            got = orecv[block : block + span, :].astype(F32)
-            rows.append(part + got[start - block : start - block + 2 * capacity])
-        rs_send[z] = jnp.concatenate(rows, axis=0).astype(BF16)
-    rs_copies = []
-    for n, (j, i) in enumerate(chip_offsets):
-        there = chip_at(j, i)
-        copy = remote(rs_send.at[there], rs_recv.at[n], me_e, there * 2 + core)
-        copy.start()
-        rs_copies.append(copy)
-    total = rs_send[chip].astype(F32)
-    for n, copy in enumerate(rs_copies):
-        copy.wait_recv()
-        total = total + rs_recv[n].astype(F32)
-    for e in range(experts):
-        part = total[e * 2 * capacity : (e + 1) * 2 * capacity]
-        ret_send[e] = stack_halves(part).astype(BF16)
-    ret_copies = []
-    for k in range(experts):
-        expert = expert_at(k)
-        for rep in (me_r, other_core):
-            if k == 0 and rep is me_r:
-                continue
-            copy = remote(ret_send.at[expert], ret.at[core, me_e], expert, rep)
-            copy.start()
-            ret_copies.append(copy)
-    ret[core, me_e] = ret_send[me_e]
-    weightings = [
-        placing_of(ids, wts, 2 * q + core, capacity, lanes)[1][:, : experts * span]
-        for q in range(2)
-    ]
-    for copy in ret_copies:
+    for copy in mix_copies:
         copy.wait_recv()
     for h in range(2):
-        rows = ret[h].astype(F32).reshape(experts * span, quarter)
+        total = mix_recv[h].astype(F32)
+        for z in range(1, chips):
+            total = total + mix_recv[2 * z + h].astype(F32)
         for q in range(2):
             start = h * half + q * quarter
-            mixed_ref[:, start : start + quarter] = dot(
-                weightings[q], rows, precision=lax.Precision.HIGHEST
-            ).astype(BF16)
-
+            rows = total[q * count : (q + 1) * count]
+            mixed_ref[:, start : start + quarter] = rows.astype(BF16)
+
+    slope_out.wait()
     cot_out.wait()
-    sent = [x_pair, g_pair, o_pair] + metas + x_forward + g_forward + rs_copies + ret_copies
+    sent = [x_pair, g_pair, o_pair] + metas + x_forward + g_forward + mix_copies
     sent += list(x_chips.values()) + list(g_chips.values())
-    for _, flying in x_sent + g_sent:
+    for _, flying in x_sent + g_sent + returning:
         sent += flying
     for copy in sent:
         copy.wait_send()
 
 
-def round_kernel(hidden_ref, cot_ref, round_ref, step_ref, out_ref):
+def round_kernel(hidden_ref, cot_ref, slope_ref, out_ref):
     hidden = hidden_ref[...]
     half = cot_ref.shape[3]
     for h in range(2):
         columns = slice(h * half, (h + 1) * half)
-        soft = jax.nn.sigmoid(round_ref[0, :, columns].astype(F32))
         grad = dot(hidden, cot_ref[h].reshape(-1, half), ((0,), (0,)))
-        out_ref[0, :, columns] = grad * step_ref[:, columns] * soft * (1.0 - soft)
+        out_ref[0, :, columns] = grad * slope_ref[:, columns].astype(F32)
 
 
 def fused_body(
@@ -390,18 +403,19 @@
     pairs = chips // 2
     rows = reps * experts * capacity
     copies = 2 + (reps - 1) + 2 * (chips - 1) + 2 * pairs * (experts - 1)
-    copies += 2 * pairs + 1 + (chips - 1) + 2 * experts
+    copies += 2 * pairs + 1 + pairs * (experts - 1) + reps - 1
     vmem = pl.BlockSpec(memory_space=pltpu.VMEM)
     anywhere = pl.BlockSpec(memory_space=pl.ANY)
-    mixed, hidden, cot = pl.pallas_call(
+    mixed, hidden, cot, slope = pl.pallas_call(
         functools.partial(layer_kernel, experts, reps),
         out_shape=(
             jax.ShapeDtypeStruct((count, width), BF16),
             jax.ShapeDtypeStruct((rows, hidden_width), BF16),
             jax.ShapeDtypeStruct((2, pairs * experts, span, half), BF16),
+            jax.ShapeDtypeStruct((hidden_width, width), BF16),
         ),
         in_specs=[vmem] * 7 + [anywhere] * 4,
-        out_specs=(vmem, vmem, anywhere),
+        out_specs=(vmem, vmem, anywhere, anywhere),
         scratch_shapes=[
             pltpu.VMEM((width, hidden_width), BF16),
             pltpu.VMEM((width, hidden_width), BF16),
@@ -421,11 +435,11 @@
             pltpu.VMEM((rows, half), BF16),
             pltpu.VMEM((rows, half), BF16),
             pltpu.VMEM((rows, half), F32),
-            pltpu.VMEM((chips, experts * 2 * capacity, half), BF16),
-            pltpu.VMEM((chips - 1, experts * 2 * capacity, half), BF16),
-            pltpu.VMEM((experts, span, half // 2), BF16),
-            pltpu.VMEM((2, experts, span, half // 2), BF16),
-            pltpu.SemaphoreType.DMA((5,)),
+            pltpu.VMEM((pairs, experts, span, half), BF16),
+            pltpu.VMEM((pairs, experts, span, half), BF16),
+            pltpu.VMEM((pairs, 4, 2 * count, half // 2), BF16),
+            pltpu.VMEM((reps, 2 * count, half // 2), BF16),
+            pltpu.SemaphoreType.DMA((6,)),
             pltpu.SemaphoreType.DMA((copies,)),
             pltpu.SemaphoreType.DMA((copies,)),
         ],
@@ -439,8 +453,8 @@
         ),
         name="layer",
     )(
-        route_ids,
-        route_weight,
+        route_ids.T,
+        route_weight.T,
         input_float,
         input_quant,
         keep_mask,
@@ -459,18 +473,17 @@
         in_specs=[
             pl.BlockSpec((rows, tile), lambda n: (0, n)),
             pl.BlockSpec((2, pairs * experts, span, half), lambda n: (0, 0, 0, 0)),
-            pl.BlockSpec((1, tile, width), lambda n: (0, n, 0)),
-            pl.BlockSpec((1, width), lambda n: (0, 0)),
+            pl.BlockSpec((tile, width), lambda n: (n, 0)),
         ],
         out_specs=pl.BlockSpec((1, tile, width), lambda n: (0, n, 0)),
         compiler_params=pltpu.CompilerParams(vmem_limit_bytes=VMEM_LIMIT),
         cost_estimate=pl.CostEstimate(
             flops=2 * rows * width * hidden_width,
             bytes_accessed=6 * width * hidden_width,
-            transcendentals=width * hidden_width,
+            transcendentals=0,
         ),
         name="round_grad",
-    )(hidden, cot, down_round, down_step)
+    )(hidden, cot, slope)
     return (mixed, round_grad)
 
 

time: 64.9 us -> 57.7 us (0.89); the launches traced: 63.9 us -> 57.4 us
  Pallas kernels: 59.9 us -> 56.1 us
  local copies, waits for them, and re-layouts: 3.32 us -> 0.63 us
    pallas_call x1, Pallas kernels: 47.7 us -> 44.9 us  [fused_body(): pl.pallas_call(functools.partial(layer_kernel, experts, reps), out_shape=...]
    unnamed x5 -> x3, local copies, waits for them, and re-layouts: 3.32 us -> 0.63 us
    pallas_call x1, Pallas kernels: 12.3 us -> 11.2 us  [fused_body(): pl.pallas_call(round_kernel, out_shape=jax.ShapeDtypeStruct((1, hidden_wi...]
where the time goes in v2:
time: 57.7 us; the launch traced here: 57.4 us
  Pallas kernels  56.1 us (97%)
  between operations  0.65 us (1%)
  local copies, waits for them, and re-layouts  0.63 us (1%)
    pallas_call x1, Pallas kernels, fused_body(): pl.pallas_call(functools.partial(layer_kernel, experts, reps), out_shape=...  44.9 us
    pallas_call x1, Pallas kernels, fused_body(): pl.pallas_call(round_kernel, out_shape=jax.ShapeDtypeStruct((1, hidden_wi...  11.2 us

profile of v2, /device:TPU:0, one launch (start us, length us, event | category | flops | bytes accessed | tf_op | source)
XLA Modules:
  0.0 57.4 jit_solution(3940086170398705265)
XLA Ops:
  0.6 44.9 %layer.1 = (bf16[8,4096]{1,0:T(8,128)(2,1)}, bf16[128,896]{1,0:T(8,128)(2,1)}, bf16[2,8,16,2048]{3,2,1,0:T(8,128)(2,1)}, bf16[896,4096]{1,0:T(8,128)(2,1)}) custom-call(s32[2,8]{1,0:T(2,128)} %bitcast.2, f32[2,8]{1,0:T(2,128)} %bitcast.3, bf16[8,4096]{1,0:T(8,128)(2,1)} %xf_ref.1, bf16[8,4096]{1,0:T(8,128)(2,1)} %xq_ref.1, s32[8,4096]{1,0:T(8,128)} %keep_ref.1, ...), custom_call_target="tpu_custom_call" | custom-call | flops 2818572288 | bytes 29360128 | tf_op jit(solution)/shard_map/layer/pallas_call | solution.py:409
  45.6 0.0 copy-start
  45.6 11.2 %round_grad.1 = f32[1,896,4096]{2,1,0:T(8,128)} custom-call(bf16[128,896]{1,0:T(8,128)(2,1)} %get-tuple-element.7.hidden_ref, bf16[2,8,16,2048]{3,2,1,0:T(8,128)(2,1)} %get-tuple-element.8.cot_ref, bf16[896,4096]{1,0:T(8,128)(2,1)} %get-tuple-element.9.slope_ref), custom_call_target="tpu_custom_call" | custom-call | flops 939524096 | bytes 22020096 | tf_op jit(solution)/shard_map/round_grad/pallas_call | solution.py:469
  56.7 0.0 copy-done
  56.7 0.6 %copy.14 = bf16[8,4096]{1,0:T(8,128)(2,1)} copy(bf16[8,4096]{1,0:T(8,128)(2,1)S(1)} %copy-done) | data formatting | bytes 131072
Async XLA Ops:
  45.6 11.2 %copy-start = (bf16[8,4096]{1,0:T(8,128)(2,1)S(1)}, bf16[8,4096]{1,0:T(8,128)(2,1)}, u32[]{:S(2)}) copy-start(bf16[8,4096]{1,0:T(8,128)(2,1)} %get-tuple-element.12) | copy-start | bytes 196612

commit v3 on v2

--- a/solution.py
+++ b/solution.py
@@ -62,9 +62,8 @@
     base_hbm,
     round_hbm,
     mixed_ref,
+    grad_hbm,
     hidden_ref,
-    cot_hbm,
-    slope_hbm,
     wg,
     wu,
     quant,
@@ -175,10 +174,10 @@
         @pl.loop(start, stop)
         def _(n):
             rows = pl.ds(pl.multiple_of(n * 16, 16), 16)
-            soft = jax.nn.sigmoid(rounding[rows, :].astype(F32))
-            scaled = step_ref[...] * soft
-            quant[rows, :] = (quant[rows, :].astype(F32) + scaled).astype(BF16)
-            rounding[rows, :] = (scaled * (1.0 - soft)).astype(BF16)
+            t = jnp.tanh(0.5 * rounding[rows, :].astype(F32))
+            step = 0.5 * step_ref[...]
+            quant[rows, :] = (quant[rows, :].astype(F32) + (step + step * t)).astype(BF16)
+            rounding[rows, :] = (0.5 * step * (1.0 - t * t)).astype(BF16)
 
     def own_half(stacked):
         parts = []
@@ -263,8 +262,6 @@
             copy.wait_recv()
         x_forward.append(forward(pair, xr))
     quantise(chunks * (1 + pairs) // (2 + pairs), chunks)
-    slope_out = pltpu.make_async_copy(rounding, slope_hbm, load_sem.at[5])
-    slope_out.start()
     g_sent = [dispatch(0, gz, g_chips, gsend, gr, True)]
 
     loads[2].wait()
@@ -322,6 +319,29 @@
         for copy in flying:
             copy.wait_recv()
         g_forward.append(forward(pair, gr))
+    for copy in g_forward:
+        copy.wait_recv()
+    tile = 128
+    tiles = hidden_width // tile
+    grad_out = []
+
+    def round_grad(start, stop):
+        @pl.loop(start, stop)
+        def _(n):
+            rows = pl.ds(pl.multiple_of(n * tile, tile), tile)
+            for h in range(2):
+                columns = slice(h * half, (h + 1) * half)
+                grad = dot(hidden_ref[:, rows], gr[h].reshape(-1, half), ((0,), (0,)))
+                rounding[rows, columns] = (grad * rounding[rows, columns].astype(F32)).astype(BF16)
+
+        span_rows = pl.ds(start * tile, (stop - start) * tile)
+        copy = pltpu.make_async_copy(
+            rounding.at[span_rows], grad_hbm.at[span_rows], load_sem.at[4 + len(grad_out)]
+        )
+        copy.start()
+        grad_out.append(copy)
+
+    round_grad(0, tiles // 2)
     member = lax.rem(me_r, 4)
     mix_copies = []
     for j, (pair, flying) in enumerate(returning):
@@ -345,10 +365,7 @@
             copy = remote(mix_send.at[pair, there], mix_recv.at[me_r], me_e, pair * 4 + there)
             copy.start()
             mix_copies.append(copy)
-    for copy in g_forward:
-        copy.wait_recv()
-    cot_out = pltpu.make_async_copy(gr, cot_hbm, load_sem.at[4])
-    cot_out.start()
+    round_grad(tiles // 2, tiles)
     for copy in mix_copies:
         copy.wait_recv()
     for h in range(2):
@@ -360,23 +377,14 @@
             rows = total[q * count : (q + 1) * count]
             mixed_ref[:, start : start + quarter] = rows.astype(BF16)
 
-    slope_out.wait()
-    cot_out.wait()
+    for copy in grad_out:
+        copy.wait()
     sent = [x_pair, g_pair, o_pair] + metas + x_forward + g_forward + mix_copies
     sent += list(x_chips.values()) + list(g_chips.values())
     for _, flying in x_sent + g_sent + returning:
         sent += flying
     for copy in sent:
         copy.wait_send()
-
-
-def round_kernel(hidden_ref, cot_ref, slope_ref, out_ref):
-    hidden = hidden_ref[...]
-    half = cot_ref.shape[3]
-    for h in range(2):
-        columns = slice(h * half, (h + 1) * half)
-        grad = dot(hidden, cot_ref[h].reshape(-1, half), ((0,), (0,)))
-        out_ref[0, :, columns] = grad * slope_ref[:, columns].astype(F32)
 
 
 def fused_body(
@@ -406,17 +414,16 @@
     copies += 2 * pairs + 1 + pairs * (experts - 1) + reps - 1
     vmem = pl.BlockSpec(memory_space=pltpu.VMEM)
     anywhere = pl.BlockSpec(memory_space=pl.ANY)
-    mixed, hidden, cot, slope = pl.pallas_call(
+    mixed, grad = pl.pallas_call(
         functools.partial(layer_kernel, experts, reps),
         out_shape=(
             jax.ShapeDtypeStruct((count, width), BF16),
-            jax.ShapeDtypeStruct((rows, hidden_width), BF16),
-            jax.ShapeDtypeStruct((2, pairs * experts, span, half), BF16),
             jax.ShapeDtypeStruct((hidden_width, width), BF16),
         ),
         in_specs=[vmem] * 7 + [anywhere] * 4,
-        out_specs=(vmem, vmem, anywhere, anywhere),
+        out_specs=(vmem, anywhere),
         scratch_shapes=[
+            pltpu.VMEM((rows, hidden_width), BF16),
             pltpu.VMEM((width, hidden_width), BF16),
             pltpu.VMEM((width, hidden_width), BF16),
             pltpu.VMEM((hidden_width, width), BF16),
@@ -447,7 +454,7 @@
             collective_id=0, has_side_effects=True, vmem_limit_bytes=VMEM_LIMIT
         ),
         cost_estimate=pl.CostEstimate(
-            flops=6 * rows * width * hidden_width,
+            flops=8 * rows * width * hidden_width,
             bytes_accessed=8 * width * hidden_width,
             transcendentals=width * hidden_width,
         ),
@@ -465,26 +472,7 @@
         down_base,
         down_round,
     )
-    tile = 128
-    round_grad = pl.pallas_call(
-        round_kernel,
-        out_shape=jax.ShapeDtypeStruct((1, hidden_width, width), F32),
-        grid=(hidden_width // tile,),
-        in_specs=[
-            pl.BlockSpec((rows, tile), lambda n: (0, n)),
-            pl.BlockSpec((2, pairs * experts, span, half), lambda n: (0, 0, 0, 0)),
-            pl.BlockSpec((tile, width), lambda n: (n, 0)),
-        ],
-        out_specs=pl.BlockSpec((1, tile, width), lambda n: (0, n, 0)),
-        compiler_params=pltpu.CompilerParams(vmem_limit_bytes=VMEM_LIMIT),
-        cost_estimate=pl.CostEstimate(
-            flops=2 * rows * width * hidden_width,
-            bytes_accessed=6 * width * hidden_width,
-            transcendentals=0,
-        ),
-        name="round_grad",
-    )(hidden, cot, slope)
-    return (mixed, round_grad)
+    return (mixed, grad.astype(F32)[None])
 
 
 def local_slots(route_ids, experts):

time: 57.7 us -> 57.1 us (0.990)
  Pallas kernels: 56.1 us -> 45.1 us
  other arithmetic: 0 us -> 10.6 us
    pallas_call x1 -> x0, Pallas kernels: 11.2 us -> none  [fused_body(): pl.pallas_call(round_kernel, out_shape=jax.ShapeDtypeStruct((1, hidden_wi...]
    broadcast_in_dim x0 -> x1, other arithmetic: none -> 10.6 us  [fused_body(): return (mixed, grad.astype(F32)[None])]
where the time goes in v3:
time: 57.1 us; the launch traced here: 56.9 us
  Pallas kernels  45.1 us (79%)
  other arithmetic  10.6 us (19%)
  between operations  0.65 us (1%)
  local copies, waits for them, and re-layouts  0.63 us (1%)
    pallas_call x1, Pallas kernels, fused_body(): pl.pallas_call(functools.partial(layer_kernel, experts, reps), out_shape=...  45.1 us
    broadcast_in_dim x1, other arithmetic, fused_body(): return (mixed, grad.astype(F32)[None])  10.6 us

profile of v3, /device:TPU:0, one launch (start us, length us, event | category | flops | bytes accessed | tf_op | source)
XLA Modules:
  0.0 56.9 jit_solution(11815574700967581843)
XLA Ops:
  0.6 45.1 %layer.1 = (bf16[8,4096]{1,0:T(8,128)(2,1)}, bf16[896,4096]{1,0:T(8,128)(2,1)}) custom-call(s32[2,8]{1,0:T(2,128)} %bitcast.5, f32[2,8]{1,0:T(2,128)} %bitcast.6, bf16[8,4096]{1,0:T(8,128)(2,1)} %xf_ref.1, bf16[8,4096]{1,0:T(8,128)(2,1)} %xq_ref.1, s32[8,4096]{1,0:T(8,128)} %keep_ref.1, bf16[8,4096]{1,0:T(8,128)(2,1)} %grad_ref.1, f32[1,4096]{1,0:T(1,128)} %step_ref.1, ...), custom_call_target="tpu_custom_call" | custom-call | flops 3758096384 | bytes 29360128 | tf_op jit(solution)/shard_map/layer/pallas_call | solution.py:417
  45.7 0.0 copy-start
  45.7 10.6 %bitcast_convert_fusion = f32[1,896,4096]{2,1,0:T(8,128)} fusion(bf16[896,4096]{1,0:T(8,128)(2,1)} %get-tuple-element.5), kind=kLoop, calls=%fused_computation | loop fusion | flops 3670016 | bytes 22020096 | tf_op jit(solution)/shard_map/broadcast_in_dim | solution.py:475
  56.3 0.0 copy-done
  56.3 0.6 %copy.14 = bf16[8,4096]{1,0:T(8,128)(2,1)} copy(bf16[8,4096]{1,0:T(8,128)(2,1)S(1)} %copy-done) | data formatting | bytes 131072
Async XLA Ops:
  45.7 10.6 %copy-start = (bf16[8,4096]{1,0:T(8,128)(2,1)S(1)}, bf16[8,4096]{1,0:T(8,128)(2,1)}, u32[]{:S(2)}) copy-start(bf16[8,4096]{1,0:T(8,128)(2,1)} %get-tuple-element.8) | copy-start | bytes 196612
